TPU v7x, 32 devices: a whole 2x2x4 slice. The times are simulated.
32 devices in a mesh: chan: 8 (over z, y), vox: 4 (over x, core).
Axes of the slice: x: 2, y: 2, z: 4, core: 2. Of those that a mesh axis runs over, the one named last changes fastest.
Arguments:
- spectra: bfloat16 [2, 512, 2048], P(None, ('chan', 'vox')), may hold values from -6 to 6
- pair_mask: int32 [8, 2], P('chan'), may hold values 0 or 1
- send_rows: int32 [32, 2, 32, 32], P(('chan', 'vox')), may hold values from 0 to 1023
- footprint: int32 [8192, 4, 8], P(('chan', 'vox')), may hold values from 0 to 2047
- kernels: bfloat16 [4, 512, 256], replicated, may hold values from -0.125 to 0.125
Outputs:
- power_map: float32 [8192, 256], P(('chan', 'vox'))
Inputs may be any that keep to these rules, and one draw needn't show every extreme that they name: `send_rows`: local lag-row indices of one offset on the sending device. `footprint`: slots of the receiving device, numbered (offset 32 + sender) * 32 + slot.
All inputs are finite; a program needn't handle non-finite values. No bound on the sum of `pair_mask` on one device may be relied on, other than what follows from the above.
Results may differ from a plain program's by a relative error of at most 0.015.
Values may be sent and summed in bfloat16 or wider, within the bound.
A program may use at most 64 MiB of HBM per device.

v0:
```python
import math

import jax
import jax.numpy as jnp
from jax import lax
from jax.sharding import PartitionSpec as P


def from_behind(array, axis, by):
    devices = lax.axis_size(axis)
    return lax.ppermute(array, axis, [(i, (i + by) % devices) for i in range(devices)])


def whiten(spectra):
    real_part = spectra[0].astype(jnp.float32)
    imag_part = spectra[1].astype(jnp.float32)
    inverse_mag = 1.0 / jnp.sqrt(real_part * real_part + imag_part * imag_part + 0.25)
    return jnp.stack([real_part * inverse_mag, imag_part * inverse_mag]).astype(jnp.bfloat16)


def phase_table(bins, lags):
    bin_index = jnp.arange(bins, dtype=jnp.int32)[:, None]
    lag_index = jnp.arange(lags, dtype=jnp.int32)[None, :] - lags // 2
    phase_index = bin_index * lag_index % bins
    angles = phase_index.astype(jnp.float32) * (2.0 * math.pi / bins)
    norm_factor = 1.0 / math.sqrt(bins)
    return jnp.concatenate(
        [jnp.cos(angles) * norm_factor, -jnp.sin(angles) * norm_factor], 0
    ).astype(jnp.bfloat16)


def form_lags(first_set, second_set, lag_table):
    first_real = first_set[0].astype(jnp.float32)[:, None, :]
    first_imag = first_set[1].astype(jnp.float32)[:, None, :]
    second_real = second_set[0].astype(jnp.float32)[None, :, :]
    second_imag = second_set[1].astype(jnp.float32)[None, :, :]
    cross_real = first_real * second_real + first_imag * second_imag
    cross_imag = first_imag * second_real - first_real * second_imag
    stacked = jnp.concatenate([cross_real, cross_imag], -1).astype(jnp.bfloat16)
    stacked = stacked.reshape(-1, stacked.shape[-1])
    return jnp.dot(stacked, lag_table, preferred_element_type=jnp.float32)


def local(spectra, pair_mask, send_rows, footprint, kernels):
    whitened = whiten(spectra)
    lag_count = kernels.shape[1]
    lag_table = phase_table(spectra.shape[2], lag_count)
    offsets = pair_mask.shape[1]
    n_vox = lax.axis_size("vox")
    shares = whitened[None]
    gathered = lax.all_gather(shares, "vox", axis=2, tiled=True)
    far_blocks = []
    for offset in range(offsets):
        far_blocks.append(from_behind(gathered[0], "chan", -(offset + 1)))
    pair_count = whitened.shape[1] * whitened.shape[1] * n_vox
    outgoing = []
    for offset in range(offsets):
        partner_block = far_blocks[offset]
        lags_here = lax.cond(
            pair_mask[0, offset] > 0,
            lambda: form_lags(whitened, partner_block, lag_table).astype(jnp.bfloat16),
            lambda: jnp.zeros((pair_count, lag_count), jnp.bfloat16),
        )
        sending = jnp.take(lags_here, send_rows[0, offset], axis=0)
        outgoing.append(sending)
    received = lax.all_to_all(
        jnp.stack(outgoing), ("chan", "vox"), split_axis=1, concat_axis=1, tiled=True
    )
    flattened = received.reshape(-1, lag_count)
    picked = jnp.take(flattened, footprint.reshape(-1), axis=0)
    picked = picked.reshape(footprint.shape + (lag_count,))
    summed = jnp.sum(picked.astype(jnp.float32), axis=2).astype(jnp.bfloat16)
    return lax.dot_general(
        summed, kernels, (((1, 2), (0, 1)), ((), ())), preferred_element_type=jnp.float32
    )


def solution(mesh):
    return jax.shard_map(
        local,
        mesh=mesh,
        in_specs=(
            P(None, ("chan", "vox"), None),
            P("chan", None),
            P(("chan", "vox"), None, None, None),
            P(("chan", "vox"), None, None),
            P(),
        ),
        out_specs=P(("chan", "vox"), None),
        check_vma=False,
    )
```

profile of v0, /device:TPU:0, one launch (start us, length us, event | category | flops | bytes accessed | tf_op | source)
XLA Modules:
  0.0 165.7 jit_solution(15170771944915535152)
XLA Ops:
  0.0 0.0 copy-start
  0.0 0.0 copy-start.4
  0.0 1.0 fusion.26
  1.1 9.1 %all_gather.3 = bf16[1,2,64,2048]{3,2,1,0:T(8,128)(2,1)} all-gather(bf16[1,2,16,2048]{3,2,1,0:T(8,128)(2,1)S(1)} %pad_maximum_fusion.3), channel_id=1, replica_groups=mesh['chan'=8,'vox'=4] {'vox'}, dimensions={2}, use_global_device_ids=true | all-gather | bytes 655360 | tf_op jit(solution)/shard_map/all_gather | solution.py:51
  10.1 4.6 %collective-permute-start = (bf16[2,64,2048]{2,1,0:T(8,128)(2,1)}, bf16[2,64,2048]{2,1,0:T(8,128)(2,1)}, u32[]{:S(2)}, u32[]{:S(2)}) collective-permute-start(bf16[2,64,2048]{2,1,0:T(8,128)(2,1)} %bitcast.16), channel_id=1, source_target_pairs={{0,28},{4,0},{8,4},{12,8},{16,12},{20,16},{24,20},{28,24},{1,29},{... | collective-permute-start | bytes 1572872 | tf_op jit(solution)/shard_map/ppermute | solution.py:11
  14.7 0.4 collective-permute-start.1
  15.2 0.7 compare_select_fusion.3
  15.9 0.7 compare_and_fusion.2
  16.7 18.3 %multiply_convert_fusion.1 = (bf16[2048,512]{1,0:T(8,128)(2,1)S(1)}, bf16[2048,512]{1,0:T(8,128)(2,1)}) fusion(s32[512]{0:T(512)S(1)} %iota_add_fusion), kind=kLoop, calls=%fused_computation.36 | loop fusion | flops 19922944 | bytes 4196352 | tf_op jit(solution)/shard_map/convert.19
  34.9 0.0 copy-done.4
  34.9 0.6 fusion.28
  36.2 0.1 reshape.201
  36.9 0.1 reshape.205
  37.0 3.8 %pad_maximum_fusion = bf16[4096,512]{1,0:T(8,128)(2,1)} fusion(bf16[2048,512]{1,0:T(8,128)(2,1)} %get-tuple-element.49, bf16[2048,512]{1,0:T(8,128)(2,1)S(1)} %get-tuple-element.48), kind=kLoop, calls=%fused_computation.34 | loop fusion | flops 8388608 | bytes 8388608 | tf_op jit(solution)/shard_map/concatenate | solution.py:27
  40.8 0.0 collective-permute-done
  40.8 8.2 %conditional.2 = (bf16[1024,512]{1,0:T(8,128)(2,1)S(1)}) conditional(s32[]{:T(128)} %bitcast.13, () %tuple.18, (bf16[2,16,2048]{2,1,0:T(8,128)(2,1)S(1)}, bf16[2,64,2048]{2,1,0:T(8,128)(2,1)}, bf16[4096,512]{1,0:T(8,128)(2,1)}) %tuple.19), branch_computations={%region_0.1_spmd, %region_1.2_spmd} | conditional | flops 4329373696 | bytes 42074148 | solution.py:59
  40.8 1.1 bitcast_convert_fusion.1
  42.0 0.0 copy-start.1
  42.0 2.6 %add_convert_fusion = (bf16[16,64,2048]{2,1,0:T(8,128)(2,1)S(1)}, bf16[16,64,2048]{2,1,0:T(8,128)(2,1)S(1)}) fusion(f32[64,2048]{1,0:T(8,128)S(1)} %get-tuple-element.33, f32[16,2048]{1,0:T(8,128)S(1)} %get-tuple-element.35, f32[64,2048]{1,0:T(8,128)S(1)} %get-tuple-element.32, f32[16,2048]{1,0:T(8,128)S(1)} %get-tuple-element.34), kind=kLoop, calls=%fused_computation.8 | loop fusion | flops 16777216 | bytes 9699328 | tf_op jit(solution)/shard_map/convert.8
  44.6 0.0 copy-done.1
  44.6 4.5 %fusion.4 = bf16[1024,512]{1,0:T(8,128)(2,1)S(1)} fusion(bf16[4096,512]{1,0:T(8,128)(2,1)S(1)} %copy-done.1, bf16[1024,2048]{1,0:T(8,128)(2,1)S(1)} %bitcast.58, bf16[1024,2048]{1,0:T(8,128)(2,1)S(1)} %bitcast.57), kind=kOutput, calls=%fused_computation.9 | convolution fusion | flops 4312268800 | bytes 13631488 | tf_op jit(solution)/shard_map/cond/branch_1_fun/dot_general | solution.py:41
  49.1 4.0 %gather_fusion.1 = bf16[1024,512]{1,0:T(8,128)(2,1)S(1)} fusion(bf16[1024,512]{1,0:T(8,128)(2,1)S(1)} %get-tuple-element.54, s32[1024]{0:T(1024)S(1)} %broadcast_clamp_fusion.2), kind=kCustom, calls=%fused_computation.clone | custom fusion | bytes 2101248 | tf_op jit(solution)/shard_map/jit(_take)/gather | solution.py:64
  53.0 0.0 collective-permute-done.1
  53.0 8.2 %conditional.3 = (bf16[1024,512]{1,0:T(8,128)(2,1)S(1)}) conditional(s32[]{:T(128)} %bitcast.20, () %tuple.20, (bf16[2,16,2048]{2,1,0:T(8,128)(2,1)S(1)}, bf16[2,64,2048]{2,1,0:T(8,128)(2,1)}, bf16[4096,512]{1,0:T(8,128)(2,1)}) %tuple.21), branch_computations={%region_2.4_spmd, %region_3.5_spmd} | conditional | flops 4329373696 | bytes 42074148 | solution.py:59
  53.1 1.1 bitcast_convert_fusion.5
  54.2 0.0 copy-start.2
  54.2 2.5 %add_convert_fusion.1 = (bf16[16,64,2048]{2,1,0:T(8,128)(2,1)S(1)}, bf16[16,64,2048]{2,1,0:T(8,128)(2,1)S(1)}) fusion(f32[64,2048]{1,0:T(8,128)S(1)} %get-tuple-element.39, f32[16,2048]{1,0:T(8,128)S(1)} %get-tuple-element.41, f32[64,2048]{1,0:T(8,128)S(1)} %get-tuple-element.38, f32[16,2048]{1,0:T(8,128)S(1)} %get-tuple-element.40), kind=kLoop, calls=%fused_computation.20 | loop fusion | flops 16777216 | bytes 9699328 | tf_op jit(solution)/shard_map/convert.16
  56.7 0.0 copy-done.2
  56.8 4.5 %fusion.12 = bf16[1024,512]{1,0:T(8,128)(2,1)S(1)} fusion(bf16[4096,512]{1,0:T(8,128)(2,1)S(1)} %copy-done.2, bf16[1024,2048]{1,0:T(8,128)(2,1)S(1)} %bitcast.60, bf16[1024,2048]{1,0:T(8,128)(2,1)S(1)} %bitcast.59), kind=kOutput, calls=%fused_computation.21 | convolution fusion | flops 4312268800 | bytes 13631488 | tf_op jit(solution)/shard_map/cond/branch_1_fun/dot_general | solution.py:41
  61.2 5.1 %gather_fusion.2 = bf16[1024,512]{1,0:T(8,128)(2,1)} fusion(bf16[1024,512]{1,0:T(8,128)(2,1)S(1)} %get-tuple-element.55, s32[1024]{0:T(1024)S(1)} %broadcast_clamp_fusion.1), kind=kCustom, calls=%fused_computation.1.clone | custom fusion | bytes 2101248 | tf_op jit(solution)/shard_map/jit(_take)/gather | solution.py:64
  66.3 1.5 select_bitcast_fusion
  67.8 0.0 copy-start.3
  67.8 1.5 pad_maximum_fusion.1
  69.3 3.5 %all-to-all-start = ((bf16[2,32,32,512]{3,2,0,1:T(8,128)(2,1)}), bf16[2,32,32,512]{3,2,0,1:T(8,128)(2,1)}, u32[]{:S(2)}, u32[]{:S(2)}) async-start(bf16[2,32,32,512]{3,2,0,1:T(8,128)(2,1)} %pad_maximum_fusion.1), calls=%async_computation | async-start | bytes 4194304 | tf_op jit(solution)/shard_map/all_to_all | solution.py:66
  72.8 0.0 copy-done.3
  72.8 0.2 copy.11
  73.0 0.5 reshape.162
  73.6 0.3 copy.9
  73.9 47.8 %all-to-all-done = bf16[2,32,32,512]{3,2,0,1:T(8,128)(2,1)} async-done(((bf16[2,32,32,512]{3,2,0,1:T(8,128)(2,1)}), bf16[2,32,32,512]{3,2,0,1:T(8,128)(2,1)}, u32[]{:S(2)}, u32[]{:S(2)}) %all-to-all-start) | async-done | bytes 2097184 | tf_op jit(solution)/shard_map/all_to_all | solution.py:66
  121.7 1.7 %copy.10 = bf16[2,32,32,512]{3,2,1,0:T(8,128)(2,1)S(1)} copy(bf16[2,32,32,512]{3,2,0,1:T(8,128)(2,1)} %all-to-all-done) | data formatting | bytes 4194304 | tf_op jit(solution)/shard_map/all_to_all | solution.py:66
  123.4 33.8 %gather_fusion = bf16[8192,512]{1,0:T(8,128)(2,1)} fusion(bf16[2048,512]{1,0:T(8,128)(2,1)S(1)} %bitcast.56, s32[8192]{0:T(1024)S(1)} %broadcast_clamp_fusion), kind=kCustom, calls=%fused_computation.2 | custom fusion | bytes 16809984 | tf_op jit(solution)/shard_map/jit(_take)/gather | solution.py:70
  157.2 7.3 %select_reduce_fusion = bf16[256,4,512]{2,1,0:T(4,128)(2,1)S(1)} fusion(pred[256,4,8]{2,1,0:T(4,128)(4,1)S(1)} %copy.9, bf16[8192,512]{1,0:T(8,128)(2,1)} %gather_fusion), kind=kLoop, calls=%fused_computation.27 | loop fusion | flops 7864320 | bytes 9445376 | tf_op jit(solution)/shard_map/reduce_sum | solution.py:72
  164.5 0.0 copy-done
  164.5 1.2 convolution_bitcast_fusion
  (10 shorter events, 0.1 us)
Async XLA Ops:
  0.0 164.5 %copy-start = (bf16[4,512,256]{2,1,0:T(8,128)(2,1)S(1)}, bf16[4,512,256]{2,1,0:T(8,128)(2,1)}, u32[]{:S(2)}) copy-start(bf16[4,512,256]{2,1,0:T(8,128)(2,1)} %param.15) | copy-start | bytes 3145732
  0.0 34.9 %copy-start.4 = (s32[1,2]{1,0:T(1,128)S(1)}, s32[1,2]{1,0:T(1,128)}, u32[]{:S(2)}) copy-start(s32[1,2]{1,0:T(1,128)} %param.12) | copy-start | bytes 28
  10.1 30.7 %collective-permute-start = (bf16[2,64,2048]{2,1,0:T(8,128)(2,1)}, bf16[2,64,2048]{2,1,0:T(8,128)(2,1)}, u32[]{:S(2)}, u32[]{:S(2)}) collective-permute-start(bf16[2,64,2048]{2,1,0:T(8,128)(2,1)} %bitcast.16), channel_id=1, source_target_pairs={{0,28},{4,0},{8,4},{12,8},{16,12},{20,16},{24,20},{28,24},{1,29},{... | collective-permute-start | bytes 1572872 | tf_op jit(solution)/shard_map/ppermute | solution.py:11
  14.7 38.3 %collective-permute-start.1 = (bf16[2,64,2048]{2,1,0:T(8,128)(2,1)}, bf16[2,64,2048]{2,1,0:T(8,128)(2,1)}, u32[]{:S(2)}, u32[]{:S(2)}) collective-permute-start(bf16[2,64,2048]{2,1,0:T(8,128)(2,1)} %bitcast.16), channel_id=1, source_target_pairs={{0,24},{4,28},{8,0},{12,4},{16,8},{20,12},{24,16},{28,20},{1,25},{... | collective-permute-start | bytes 1572872 | tf_op jit(solution)/shard_map/ppermute | solution.py:11
  42.0 2.6 %copy-start.1 = (bf16[4096,512]{1,0:T(8,128)(2,1)S(1)}, bf16[4096,512]{1,0:T(8,128)(2,1)}, u32[]{:S(2)}) copy-start(bf16[4096,512]{1,0:T(8,128)(2,1)} %get-tuple-element.26) | copy-start | bytes 12582916 | tf_op jit(solution)/shard_map/cond
  54.2 2.5 %copy-start.2 = (bf16[4096,512]{1,0:T(8,128)(2,1)S(1)}, bf16[4096,512]{1,0:T(8,128)(2,1)}, u32[]{:S(2)}) copy-start(bf16[4096,512]{1,0:T(8,128)(2,1)} %get-tuple-element.29) | copy-start | bytes 12582916 | tf_op jit(solution)/shard_map/cond
  67.8 5.0 %copy-start.3 = (s32[256,4,8]{0,2,1:T(8,128)S(1)}, s32[256,4,8]{0,2,1:T(8,128)}, u32[]{:S(2)}) copy-start(s32[256,4,8]{0,2,1:T(8,128)} %param.14) | copy-start | bytes 98308
  69.3 52.4 %all-to-all-start = ((bf16[2,32,32,512]{3,2,0,1:T(8,128)(2,1)}), bf16[2,32,32,512]{3,2,0,1:T(8,128)(2,1)}, u32[]{:S(2)}, u32[]{:S(2)}) async-start(bf16[2,32,32,512]{3,2,0,1:T(8,128)(2,1)} %pad_maximum_fusion.1), calls=%async_computation | async-start | bytes 4194304 | tf_op jit(solution)/shard_map/all_to_all | solution.py:66
where the time goes:
time: 166 us
  waiting for transfers between devices  47.8 us (29%)
  local copies, waits for them, and re-layouts  46.3 us (28%)
  other arithmetic  42.4 us (26%)
  matrix products  10.1 us (6%)
  blocking collectives  9.08 us (5%)
  starting transfers between devices  8.49 us (5%)
    all_to_all x1, waiting for transfers between devices, local(): lax.all_to_all(jnp.stack(outgoing), ('chan', 'vox'), split_axis=1, concat...  47.8 us
    gather x1, local copies, waits for them, and re-layouts, local(): picked = jnp.take(flattened, footprint.reshape(-1), axis=0)  33.8 us
    another operation x4, other arithmetic  24.4 us
    all_gather x1, blocking collectives, local(): gathered = lax.all_gather(shares, 'vox', axis=2, tiled=True)  9.08 us
    gather x2, local copies, waits for them, and re-layouts, local(): sending = jnp.take(lags_here, send_rows[0, offset], axis=0)  9.03 us
    dot_general x2, matrix products, form_lags(): return jnp.dot(stacked, lag_table, preferred_element_type=jnp.float32)  8.96 us
    reduce_sum x1, other arithmetic, local(): summed = jnp.sum(picked.astype(jnp.float32), axis=2).astype(jnp.bfloat16)  7.33 us
    ppermute x2, starting transfers between devices, from_behind(): lax.ppermute(array, axis, [(i, (i + by) % devices) for i in range(devices)])  5.01 us
  transfers between devices with their start and end apart: 3, of which 1 were waited for; matrix products, arithmetic and copies ran while one was open for 23% of the time, Pallas kernels for 0%

commit v1 on v0

v1 whole, which is shorter than its diff:
```python
import functools
import math

import jax
import jax.numpy as jnp
import numpy as np
from jax import lax
from jax.experimental import pallas as pl
from jax.experimental.pallas import tpu as pltpu
from jax.sharding import PartitionSpec as P

MESH = pl.DeviceIdType.MESH
LANES = 128


def whiten(spectra):
    real_part = spectra[0].astype(jnp.float32)
    imag_part = spectra[1].astype(jnp.float32)
    inverse_mag = 1.0 / jnp.sqrt(real_part * real_part + imag_part * imag_part + 0.25)
    return jnp.stack([real_part * inverse_mag, imag_part * inverse_mag]).astype(jnp.bfloat16)


def phase_table(bins, lags):
    bin_index = np.arange(bins, dtype=np.int64)[:, None]
    lag_index = np.arange(lags, dtype=np.int64)[None, :] - lags // 2
    phase_index = bin_index * lag_index % bins
    angles = phase_index.astype(np.float32) * np.float32(2.0 * math.pi / bins)
    norm_factor = np.float32(1.0 / math.sqrt(bins))
    table = np.concatenate([np.cos(angles) * norm_factor, -np.sin(angles) * norm_factor], 0)
    return jnp.asarray(table.astype(jnp.bfloat16))


def kernel(dims, own, feet, table_hbm, kern, out, held, table, counts, lags, send_sem, recv_sem, load_sem):
    n_chan, n_vox, per_dev, bins, offsets, cap = dims
    n_dev = n_chan * n_vox
    depth = n_chan // 2
    chan, vox = lax.axis_index("chan"), lax.axis_index("vox")
    hi, lo = chan // 2, chan % 2
    far, core = vox // 2, vox % 2
    me = chan * n_vox + vox

    def chan_at(d, flip):
        l = 1 - lo if flip else lo
        return lax.rem(hi + depth - d, depth) * 2 + l

    def vox_at(flip_x, flip_core):
        f = 1 - far if flip_x else far
        c = 1 - core if flip_core else core
        return f * 2 + c

    def source(d, flip_y, flip_x, flip_core):
        return chan_at(d, flip_y) * n_vox + vox_at(flip_x, flip_core)

    load = pltpu.make_async_copy(table_hbm, table, load_sem)
    load.start()

    barrier = pltpu.get_barrier_semaphore()
    near_y = (chan_at(0, True), vox)
    near_x = (chan, vox_at(True, False))
    near_core = (chan, vox_at(False, True))
    column = [(chan_at(depth - d, False), vox) for d in range(1, depth)]
    partners = column + [near_y, near_x, near_core]
    for device in partners:
        pl.semaphore_signal(barrier, inc=1, device_id=device, device_id_type=MESH)
    held[0, me] = own[0]
    held[1, me] = own[1]
    pl.semaphore_wait(barrier, len(partners))

    started = []

    def send(part, shard, device):
        slot = sum(1 for p, _ in started if p == part)
        copy = pltpu.make_async_remote_copy(
            src_ref=held.at[part, shard],
            dst_ref=held.at[part, shard],
            send_sem=send_sem.at[part, slot],
            recv_sem=recv_sem.at[part, shard],
            device_id=device,
            device_id_type=MESH,
        )
        copy.start()
        started.append((part, copy))

    def arrive(part, shard):
        pltpu.make_async_remote_copy(
            src_ref=held.at[part, shard],
            dst_ref=held.at[part, shard],
            send_sem=send_sem.at[part, 0],
            recv_sem=recv_sem.at[part, shard],
            device_id=near_core,
            device_id_type=MESH,
        ).wait_recv()

    rows_out, slots = feet.shape
    received = counts.shape[1]
    pieces = 4 * depth
    piece_rows = rows_out // pieces

    def count_piece(step):
        start = step * piece_rows
        slot_id = lax.broadcasted_iota(jnp.int32, (piece_rows, received), 1)
        total = jnp.zeros((piece_rows, received), jnp.float32)
        for slot in range(slots):
            total += jnp.where(slot_id == feet[pl.ds(start, piece_rows), slot : slot + 1], 1.0, 0.0)
        counts[pl.ds(start, piece_rows), :] = total.astype(jnp.bfloat16)

    first = (near_y, near_x)
    second = (near_x, near_y)
    for d in range(depth):
        for part in range(2):
            shard = source(d, False, False, False)
            if d > 0:
                arrive(part, shard)
            else:
                for device in column:
                    send(part, shard, device)
            send(part, shard, first[part])
            send(part, shard, second[part])
            send(part, shard, near_core)
        count_piece(d)
    for d in range(depth):
        for part in range(2):
            shard = source(d, part == 0, part == 1, False)
            arrive(part, shard)
            send(part, shard, second[part])
            send(part, shard, near_core)
        count_piece(depth + d)
    for d in range(depth):
        for part in range(2):
            shard = source(d, part == 1, part == 0, False)
            arrive(part, shard)
            send(part, shard, near_core)
        count_piece(2 * depth + d)
    for d in range(depth):
        for part in range(2):
            shard = source(d, True, True, False)
            arrive(part, shard)
            send(part, shard, near_core)
        count_piece(3 * depth + d)
    load.wait()
    for flip_y, flip_x in ((False, False), (True, False), (False, True), (True, True)):
        for d in range(depth):
            for part in range(2):
                arrive(part, source(d, flip_y, flip_x, True))
    for _, copy in started:
        copy.wait_send()

    per_receiver = offsets * cap
    in_row = LANES // per_receiver
    my_row, my_lane = me // in_row, lax.rem(me, in_row) * per_receiver
    block = n_vox * per_dev
    rows = n_vox * cap
    chunk = 512

    def numbers(part, b, k):
        tiles = held[part, pl.ds(b * n_vox, n_vox), :, bins:].astype(jnp.float32)
        row_id = lax.broadcasted_iota(jnp.int32, tiles.shape, 1)
        line = jnp.sum(jnp.where(row_id == my_row, tiles, 0.0), axis=1, keepdims=True)
        shape = (n_vox, cap, LANES)
        lane = lax.broadcasted_iota(jnp.int32, shape, 2)
        wanted = lax.broadcasted_iota(jnp.int32, shape, 1) + (my_lane + k * cap)
        picked = jnp.where(lane == wanted, jnp.broadcast_to(line, shape), 0.0)
        return jnp.sum(picked, axis=2, keepdims=True)

    def one_hot(values):
        chosen = lax.broadcasted_iota(jnp.int32, (n_vox, cap, block), 2).astype(jnp.float32)
        hot = jnp.where(chosen == values, 1.0, 0.0)
        return hot.reshape(rows, block).astype(jnp.bfloat16)

    def select(hot, part, b, at):
        channels = held[part, pl.ds(b * n_vox, n_vox), :, at : at + chunk].reshape(block, chunk)
        return jnp.dot(hot, channels, preferred_element_type=jnp.float32)

    def one_block(b, carry):
        owner = lax.broadcasted_iota(jnp.int32, (n_vox, cap, 1), 0).astype(jnp.float32) * per_dev
        mine, theirs, partner = [], [], []
        for k in range(offsets):
            mine.append(one_hot(numbers(0, b, k) + owner))
            theirs.append(one_hot(numbers(1, b, k)))
            partner.append(lax.rem(b + k + 1, n_chan))
        both = jnp.concatenate(mine, 0)
        total = jnp.zeros((offsets * rows, table.shape[1]), jnp.float32)
        for at in range(0, bins, chunk):
            re_i, im_i = select(both, 0, b, at), select(both, 1, b, at)
            re_j = jnp.concatenate([select(theirs[k], 0, partner[k], at) for k in range(offsets)], 0)
            im_j = jnp.concatenate([select(theirs[k], 1, partner[k], at) for k in range(offsets)], 0)
            cross_re = (re_i * re_j + im_i * im_j).astype(jnp.bfloat16)
            cross_im = (im_i * re_j - re_i * im_j).astype(jnp.bfloat16)
            total += jnp.dot(cross_re, table[at : at + chunk], preferred_element_type=jnp.float32)
            total += jnp.dot(
                cross_im, table[bins + at : bins + at + chunk], preferred_element_type=jnp.float32
            )
        for k in range(offsets):
            place = pl.multiple_of(k * n_dev * cap + b * rows, rows)
            lags[pl.ds(place, rows), :] = total[k * rows : (k + 1) * rows].astype(jnp.bfloat16)
        return carry

    lax.fori_loop(0, n_chan, one_block, 0)

    tiles = out.shape[0]
    power = jnp.zeros(out.shape, jnp.float32)
    for kind in range(kern.shape[0]):
        summed = jnp.dot(
            counts[kind * tiles : (kind + 1) * tiles], lags[...], preferred_element_type=jnp.float32
        ).astype(jnp.bfloat16)
        power += jnp.dot(summed, kern[kind], preferred_element_type=jnp.float32)
    out[...] = power


def local(spectra, pair_mask, send_rows, footprint, kernels):
    n_chan, n_vox = lax.axis_size("chan"), lax.axis_size("vox")
    n_dev = n_chan * n_vox
    _, per_dev, bins = spectra.shape
    kinds, lag_count, voxels = kernels.shape
    _, offsets, _, cap = send_rows.shape
    tiles, _, slots = footprint.shape
    block = n_vox * per_dev
    table = phase_table(bins, lag_count)
    order = jnp.transpose(send_rows[0], (1, 0, 2))
    own_channel = jnp.where(pair_mask[0][None, :, None] > 0, order // block, -128)
    numbers = jnp.stack([own_channel, order % block]).reshape(2, per_dev, -1)
    shard = jnp.concatenate([whiten(spectra), numbers.astype(jnp.bfloat16)], -1)
    width = shard.shape[-1]
    feet = jnp.transpose(footprint, (1, 0, 2)).reshape(kinds * tiles, slots)
    received = offsets * n_dev * cap
    sends = 4 * n_chan // 2 * 2 + n_chan * 2
    vmem = pl.BlockSpec(memory_space=pltpu.VMEM)
    return pl.pallas_call(
        functools.partial(kernel, (n_chan, n_vox, per_dev, bins, offsets, cap)),
        out_shape=jax.ShapeDtypeStruct((tiles, voxels), jnp.float32),
        in_specs=[vmem, vmem, pl.BlockSpec(memory_space=pl.ANY), vmem],
        out_specs=vmem,
        scratch_shapes=[
            pltpu.VMEM((2, n_dev, per_dev, width), jnp.bfloat16),
            pltpu.VMEM(table.shape, jnp.bfloat16),
            pltpu.VMEM((kinds * tiles, received), jnp.bfloat16),
            pltpu.VMEM((received, lag_count), jnp.bfloat16),
            pltpu.SemaphoreType.DMA((2, sends)),
            pltpu.SemaphoreType.DMA((2, n_dev)),
            pltpu.SemaphoreType.DMA,
        ],
        compiler_params=pltpu.CompilerParams(
            collective_id=0, has_side_effects=True, vmem_limit_bytes=56 * 1024 * 1024
        ),
    )(shard, feet, table, kernels)


def solution(mesh):
    return jax.shard_map(
        local,
        mesh=mesh,
        in_specs=(
            P(None, ("chan", "vox"), None),
            P("chan", None),
            P(("chan", "vox"), None, None, None),
            P(("chan", "vox"), None, None),
            P(),
        ),
        out_specs=P(("chan", "vox"), None),
        check_vma=False,
    )
```

time: 166 us -> 67.7 us (0.41)
  Pallas kernels: 0 us -> 60.4 us
  waiting for transfers between devices: 47.8 us -> 0 us
  local copies, waits for them, and re-layouts: 46.3 us -> 3.62 us
  other arithmetic: 42.4 us -> 3.09 us
  matrix products: 10.1 us -> 0 us
  blocking collectives: 9.08 us -> 0 us
  starting transfers between devices: 8.49 us -> 0 us
    pallas_call x0 -> x1, Pallas kernels: none -> 60.4 us  [local(): pl.pallas_call(functools.partial(kernel, (n_chan, n_vox, per_dev, bins, o...]
    all_to_all x1 -> x0, waiting for transfers between devices: 47.8 us -> none  [local(): lax.all_to_all(jnp.stack(outgoing), ('chan', 'vox'), split_axis=1, concat...]
    gather x3 -> x0, local copies, waits for them, and re-layouts: 42.8 us -> none  [the longest x1 33.8 us: local(): picked = jnp.take(flattened, footprint.reshape(-1), axis=0)]
    another operation x8 -> x2, other arithmetic: 27.4 us -> 1.76 us
    dot_general x3 -> x0, matrix products: 10.1 us -> none  [the longest x2 8.96 us: form_lags(): return jnp.dot(stacked, lag_table, preferred_element_type=jnp.float32)]
    all_gather x1 -> x0, blocking collectives: 9.08 us -> none  [local(): gathered = lax.all_gather(shares, 'vox', axis=2, tiled=True)]
    reduce_sum x1 -> x0, other arithmetic: 7.33 us -> none  [local(): summed = jnp.sum(picked.astype(jnp.float32), axis=2).astype(jnp.bfloat16)]
    ppermute x2 -> x0, starting transfers between devices: 5.01 us -> none  [from_behind(): lax.ppermute(array, axis, [(i, (i + by) % devices) for i in range(devices)])]
  transfers between devices with their start and end apart: 3 -> 0, of which waited for: 1 -> 0; matrix products, arithmetic and copies ran while one was open for 23% -> 0% of each run, Pallas kernels for 0% -> 0%
where the time goes in v1:
time: 67.7 us; the launch traced here: 67.1 us
  Pallas kernels  60.4 us (89%)
  local copies, waits for them, and re-layouts  3.62 us (5%)
  other arithmetic  3.09 us (5%)
    pallas_call x1, Pallas kernels, local(): pl.pallas_call(functools.partial(kernel, (n_chan, n_vox, per_dev, bins, o...  60.4 us
    another operation x2, other arithmetic  1.76 us
    transpose x1, local copies, waits for them, and re-layouts, local(): feet = jnp.transpose(footprint, (1, 0, 2)).reshape(kinds * tiles, slots)  1.74 us
    unnamed x1, local copies, waits for them, and re-layouts  1.67 us

profile of v1, /device:TPU:0, one launch (start us, length us, event | category | flops | bytes accessed | tf_op | source)
XLA Modules:
  0.0 67.1 jit_solution(11069324175916634699)
XLA Ops:
  0.0 0.7 compare_bitcast_fusion
  0.7 0.8 %fusion.6 = (bf16[32,2,32]{2,0,1:T(8,128)(2,1)S(1)}, bf16[32,2,32]{2,0,1:T(8,128)(2,1)S(1)}) fusion(s32[1,2,32,32]{3,2,1,0:T(8,128)} %param.8, pred[2]{0:T(512)(128)(4,1)S(1)} %compare_bitcast_fusion), kind=kLoop, calls=%fused_computation.16 | loop fusion | flops 45056 | bytes 16386 | tf_op jit(solution)/shard_map/convert.3
  1.5 0.1 stack.16
  1.6 0.1 stack.17
  1.7 0.9 %fusion.3 = (bf16[1,16,2048]{2,1,0:T(8,128)(2,1)S(1)}, bf16[1,16,2048]{2,1,0:T(8,128)(2,1)S(1)}) fusion(bf16[2,16,2048]{2,1,0:T(8,128)(2,1)} %param.6), kind=kLoop, calls=%fused_computation.8 | loop fusion | flops 327680 | bytes 262144 | tf_op jit(solution)/shard_map/convert.4
  2.6 0.7 maximum_maximum_fusion.own
  3.3 1.7 %copy.9 = s32[4,256,8]{2,1,0:T(8,128)} copy(s32[4,256,8]{1,2,0:T(8,128)} %bitcast.33) | data formatting | bytes 65536 | tf_op jit(solution)/shard_map/transpose | solution.py:224
  5.0 60.4 %shard_map.64 = f32[256,256]{1,0:T(8,128)} custom-call(bf16[2,16,2176]{2,1,0:T(8,128)(2,1)} %maximum_maximum_fusion.own, s32[1024,8]{1,0:T(8,128)} %bitcast.32, bf16[4096,512]{1,0:T(8,128)(2,1)} %constant.36.clone.table_hbm, bf16[4,512,256]{2,1,0:T(8,128)(2,1)} %kern.1), custom_call_target="tpu_custom_call" | custom-call | tf_op jit(solution)/shard_map/pallas_call | solution.py:228
  65.5 1.7 %copy.11 = f32[256,256]{1,0:T(8,128)} copy(f32[256,256]{1,0:T(8,128)} %shard_map.64) | data formatting | bytes 524288
  (2 shorter events, 0.0 us)

commit v2 on v1

v2 whole, which is shorter than its diff:
```python
import functools
import math

import jax
import jax.numpy as jnp
import numpy as np
from jax import lax
from jax.experimental import pallas as pl
from jax.experimental.pallas import tpu as pltpu
from jax.sharding import PartitionSpec as P

MESH = pl.DeviceIdType.MESH
LANES = 128


def whiten(spectra):
    real_part = spectra[0].astype(jnp.float32)
    imag_part = spectra[1].astype(jnp.float32)
    inverse_mag = 1.0 / jnp.sqrt(real_part * real_part + imag_part * imag_part + 0.25)
    return jnp.stack([real_part * inverse_mag, imag_part * inverse_mag]).astype(jnp.bfloat16)


def phase_table(bins, lags):
    bin_index = np.arange(bins, dtype=np.int64)[:, None]
    lag_index = np.arange(lags, dtype=np.int64)[None, :] - lags // 2
    phase_index = bin_index * lag_index % bins
    angles = phase_index.astype(np.float32) * np.float32(2.0 * math.pi / bins)
    norm_factor = np.float32(1.0 / math.sqrt(bins))
    table = np.concatenate([np.cos(angles) * norm_factor, -np.sin(angles) * norm_factor], 0)
    return jnp.asarray(table.astype(jnp.bfloat16))


def kernel(dims, *refs):
    n_chan, n_vox, per_dev, bins, offsets, cap, stages = dims
    own, refs = refs[:stages], refs[stages:]
    feet, table_hbm, out = refs[:3]
    held, refs = refs[3 : 3 + stages], refs[3 + stages :]
    table, counts, lags, partial, feet_rows, hot_i, hot_j, send_sem, recv_sem, load_sem = refs
    n_dev = n_chan * n_vox
    depth = n_chan // 2
    width = bins // stages
    chan, vox = lax.axis_index("chan"), lax.axis_index("vox")
    hi, lo = chan // 2, chan % 2
    far, core = vox // 2, vox % 2
    me = chan * n_vox + vox

    def chan_at(d, flip):
        l = 1 - lo if flip else lo
        return lax.rem(hi + depth - d, depth) * 2 + l

    def vox_at(flip_x, flip_core):
        f = 1 - far if flip_x else far
        c = 1 - core if flip_core else core
        return f * 2 + c

    def source(d, flip_y, flip_x, flip_core):
        return chan_at(d, flip_y) * n_vox + vox_at(flip_x, flip_core)

    barrier = pltpu.get_barrier_semaphore()
    near_y = (chan_at(0, True), vox)
    near_x = (chan, vox_at(True, False))
    near_core = (chan, vox_at(False, True))
    column = [(chan_at(depth - d, False), vox) for d in range(1, depth)]
    partners = column + [near_y, near_x, near_core]
    for device in partners:
        pl.semaphore_signal(barrier, inc=1, device_id=device, device_id_type=MESH)
    for stage in range(stages):
        for part in range(2):
            held[stage][part, me] = own[stage][part]
    load = pltpu.make_async_copy(table_hbm, table, load_sem)
    load.start()
    pl.semaphore_wait(barrier, len(partners))

    first = (near_y, near_x)
    second = (near_x, near_y)

    def copy(stage, part, shard, device, slot):
        return pltpu.make_async_remote_copy(
            src_ref=held[stage].at[part, shard],
            dst_ref=held[stage].at[part, shard],
            send_sem=send_sem.at[stage * 2 + part, slot],
            recv_sem=recv_sem.at[stage * 2 + part, shard],
            device_id=device,
            device_id_type=MESH,
        )

    def spread(stage, part, phase, d, shard):
        if phase == 0:
            copy(stage, part, shard, first[part], d).start()
            copy(stage, part, shard, second[part], depth + d).start()
        if phase == 1:
            copy(stage, part, shard, second[part], 2 * depth + d).start()
        copy(stage, part, shard, near_core, (3 + phase) * depth + d).start()

    def send_own(stage):
        for part in range(2):
            for d, device in enumerate(column):
                copy(stage, part, me, device, 7 * depth + d).start()
        for part in range(2):
            spread(stage, part, 0, 0, me)

    def pass_on(stage, phase, d):
        for part in range(2):
            flip_y = phase == 3 or phase == 1 + part
            flip_x = phase == 3 or phase == 2 - part
            shard = source(d, flip_y, flip_x, False)
            copy(stage, part, shard, near_core, 0).wait_recv()
            spread(stage, part, phase, d, shard)

    def finish_arrivals(stage):
        for flip_y, flip_x in ((False, False), (True, False), (False, True), (True, True)):
            def one(d, carry):
                for part in range(2):
                    shard = source(d, flip_y, flip_x, True)
                    copy(stage, part, shard, near_core, 0).wait_recv()
                return carry
            lax.fori_loop(0, depth, one, 0)

    rows_out, slots = feet_rows.shape
    kinds, tiles = feet.shape[0], feet.shape[2]
    received = counts.shape[1]
    pieces = 4 * depth
    piece_rows = rows_out // pieces

    def count_piece(step):
        start = pl.multiple_of(step * piece_rows, piece_rows)
        slot_id = lax.broadcasted_iota(jnp.int32, (piece_rows, received), 1)
        total = jnp.zeros((piece_rows, received), jnp.float32)
        for slot in range(slots):
            total += jnp.where(slot_id == feet_rows[pl.ds(start, piece_rows), slot : slot + 1], 1.0, 0.0)
        counts[pl.ds(start, piece_rows), :] = total.astype(jnp.bfloat16)

    per_receiver = offsets * cap
    in_row = LANES // per_receiver
    my_row, my_lane = me // in_row, lax.rem(me, in_row) * per_receiver
    block = n_vox * per_dev
    rows = n_vox * cap
    group_rows = 2 * offsets * rows
    span = (2 + offsets) * block
    chunk = 512

    def numbers(part, b, k):
        tiles_in = held[0][part, pl.ds(b * n_vox, n_vox), :, width:].astype(jnp.float32)
        row_id = lax.broadcasted_iota(jnp.int32, tiles_in.shape, 1)
        line = jnp.sum(jnp.where(row_id == my_row, tiles_in, 0.0), axis=1, keepdims=True)
        shape = (n_vox, cap, LANES)
        lane = lax.broadcasted_iota(jnp.int32, shape, 2)
        wanted = lax.broadcasted_iota(jnp.int32, shape, 1) + (my_lane + k * cap)
        picked = jnp.where(lane == wanted, jnp.broadcast_to(line, shape), 0.0)
        return jnp.sum(picked, axis=2, keepdims=True)

    def one_hot(values):
        chosen = lax.broadcasted_iota(jnp.int32, (n_vox, cap, span), 2).astype(jnp.float32)
        hot = jnp.where(chosen == values, 1.0, 0.0)
        return hot.reshape(rows, span).astype(jnp.bfloat16)

    def make_hot(g):
        owner = lax.broadcasted_iota(jnp.int32, (n_vox, cap, 1), 0).astype(jnp.float32) * per_dev
        for u in range(2):
            for k in range(offsets):
                at = pl.multiple_of(g * group_rows + (u * offsets + k) * rows, rows)
                hot_i[pl.ds(at, rows), :] = one_hot(numbers(0, 2 * g + u, k) + owner + u * block)
                hot_j[pl.ds(at, rows), :] = one_hot(numbers(1, 2 * g + u, k) + (u + k + 1) * block)

    def channels(stage, part, g, at):
        found = []
        for u in range(2 + offsets):
            b = lax.rem(2 * g + u, n_chan)
            piece = held[stage][part, pl.ds(b * n_vox, n_vox), :, at : at + chunk]
            found.append(piece.reshape(block, chunk))
        return jnp.concatenate(found, 0)

    def form(stage, passing):
        per_group = width // chunk
        steps = 4 * depth // ((n_chan // 2) * per_group)

        def one_group(g, carry):
            if stage == 0:
                make_hot(g)
            base = pl.multiple_of(g * group_rows, group_rows)
            pick_i, pick_j = hot_i[pl.ds(base, group_rows), :], hot_j[pl.ds(base, group_rows), :]
            total = jnp.zeros((group_rows, table.shape[1]), jnp.float32)
            for c in range(per_group):
                at = c * chunk
                re, im = channels(stage, 0, g, at), channels(stage, 1, g, at)
                re_i = jnp.dot(pick_i, re, preferred_element_type=jnp.float32)
                im_i = jnp.dot(pick_i, im, preferred_element_type=jnp.float32)
                re_j = jnp.dot(pick_j, re, preferred_element_type=jnp.float32)
                im_j = jnp.dot(pick_j, im, preferred_element_type=jnp.float32)
                cross_re = (re_i * re_j + im_i * im_j).astype(jnp.bfloat16)
                cross_im = (im_i * re_j - re_i * im_j).astype(jnp.bfloat16)
                f = stage * width + at
                total += jnp.dot(cross_re, table[f : f + chunk], preferred_element_type=jnp.float32)
                total += jnp.dot(
                    cross_im, table[bins + f : bins + f + chunk], preferred_element_type=jnp.float32
                )
                if passing:
                    step = (g * per_group + c) * steps
                    for phase in range(4):
                        @pl.when(step // depth == phase)
                        def _():
                            for i in range(steps):
                                d = lax.rem(step, depth) + i
                                if phase > 0:
                                    pass_on(stage + 1, phase, d)
                                elif i > 0:
                                    pass_on(stage + 1, 0, d)
                                else:
                                    @pl.when(d > 0)
                                    def _():
                                        pass_on(stage + 1, 0, d)
            if stage > 0:
                total += partial[pl.ds(base, group_rows), :]
            if stage < stages - 1:
                partial[pl.ds(base, group_rows), :] = total
            else:
                for u in range(2):
                    for k in range(offsets):
                        place = pl.multiple_of(k * n_dev * cap + (2 * g + u) * rows, rows)
                        at = (u * offsets + k) * rows
                        lags[pl.ds(place, rows), :] = total[at : at + rows].astype(jnp.bfloat16)
            return carry

        lax.fori_loop(0, n_chan // 2, one_group, 0)

    send_own(0)
    for kind in range(kinds):
        feet_rows[kind * tiles : (kind + 1) * tiles, :] = feet[kind].T
    for phase in range(4):
        def one(d, carry, phase=phase):
            if phase == 0:
                @pl.when(d > 0)
                def _():
                    pass_on(0, 0, d)
            else:
                pass_on(0, phase, d)
            count_piece(phase * depth + d)
            return carry
        lax.fori_loop(0, depth, one, 0)
        if phase == 1:
            for stage in range(1, stages):
                send_own(stage)
    load.wait()
    for stage in range(stages):
        finish_arrivals(stage)
        form(stage, stage + 1 < stages)

    def sent(slot, carry):
        for stage in range(stages):
            for part in range(2):
                copy(stage, part, me, near_core, slot).wait_send()
        return carry

    lax.fori_loop(0, 8 * depth - 1, sent, 0)
    for kind in range(kinds):
        out[kind] = jnp.dot(
            counts[kind * tiles : (kind + 1) * tiles], lags[...], preferred_element_type=jnp.float32
        ).astype(jnp.bfloat16)


def local(spectra, pair_mask, send_rows, footprint, kernels):
    n_chan, n_vox = lax.axis_size("chan"), lax.axis_size("vox")
    n_dev = n_chan * n_vox
    _, per_dev, bins = spectra.shape
    kinds, lag_count, voxels = kernels.shape
    _, offsets, _, cap = send_rows.shape
    tiles, _, slots = footprint.shape
    block = n_vox * per_dev
    table = phase_table(bins, lag_count)
    order = jnp.transpose(send_rows[0], (1, 0, 2))
    own_channel = jnp.where(pair_mask[0][None, :, None] > 0, order // block, -1024)
    numbers = jnp.stack([own_channel, order % block]).reshape(2, per_dev, -1)
    whitened = whiten(spectra)
    stages = 2
    width = bins // stages
    shards = [whitened[:, :, stage * width : (stage + 1) * width] for stage in range(stages)]
    shards[0] = jnp.concatenate([shards[0], numbers.astype(jnp.bfloat16)], -1)
    feet = jnp.transpose(footprint, (1, 2, 0))
    received = offsets * n_dev * cap
    span = (2 + offsets) * block
    vmem = pl.BlockSpec(memory_space=pltpu.VMEM)
    summed = pl.pallas_call(
        functools.partial(kernel, (n_chan, n_vox, per_dev, bins, offsets, cap, stages)),
        out_shape=jax.ShapeDtypeStruct((kinds, tiles, lag_count), jnp.bfloat16),
        in_specs=[vmem] * (stages + 1) + [pl.BlockSpec(memory_space=pl.ANY)],
        out_specs=vmem,
        scratch_shapes=[
            pltpu.VMEM((2, n_dev, per_dev, shard.shape[-1]), jnp.bfloat16) for shard in shards
        ]
        + [
            pltpu.VMEM(table.shape, jnp.bfloat16),
            pltpu.VMEM((kinds * tiles, received), jnp.bfloat16),
            pltpu.VMEM((received, lag_count), jnp.bfloat16),
            pltpu.VMEM((received, lag_count), jnp.float32),
            pltpu.VMEM((kinds * tiles, slots), jnp.int32),
            pltpu.VMEM((received, span), jnp.bfloat16),
            pltpu.VMEM((received, span), jnp.bfloat16),
            pltpu.SemaphoreType.DMA((2 * stages, 8 * n_chan // 2 - 1)),
            pltpu.SemaphoreType.DMA((2 * stages, n_dev)),
            pltpu.SemaphoreType.DMA,
        ],
        compiler_params=pltpu.CompilerParams(
            collective_id=0, has_side_effects=True, vmem_limit_bytes=58 * 1024 * 1024
        ),
    )(*shards, feet, table)
    return lax.dot_general(
        summed, kernels, (((0, 2), (0, 1)), ((), ())), preferred_element_type=jnp.float32
    )


def solution(mesh):
    return jax.shard_map(
        local,
        mesh=mesh,
        in_specs=(
            P(None, ("chan", "vox"), None),
            P("chan", None),
            P(("chan", "vox"), None, None, None),
            P(("chan", "vox"), None, None),
            P(),
        ),
        out_specs=P(("chan", "vox"), None),
        check_vma=False,
    )
```

time: 67.7 us -> 62.2 us (0.919)
  Pallas kernels: 60.4 us -> 55.1 us
  local copies, waits for them, and re-layouts: 3.62 us -> 0.21 us
  matrix products: 0 us -> 2.37 us
  other arithmetic: 3.09 us -> 3.77 us
    pallas_call x1, Pallas kernels: 60.4 us -> 55.1 us  [local(): pl.pallas_call(functools.partial(kernel, (n_chan, n_vox, per_dev, bins, o...]
    dot_general x0 -> x1, matrix products: none -> 2.37 us  [local(): lax.dot_general(summed, kernels, (((0, 2), (0, 1)), ((), ())), preferred_...]
    transpose x1 -> x0, local copies, waits for them, and re-layouts: 1.74 us -> none  [local(): feet = jnp.transpose(footprint, (1, 0, 2)).reshape(kinds * tiles, slots)]
    unnamed x1 -> x2, local copies, waits for them, and re-layouts: 1.67 us -> 0.01 us
    another operation x2 -> x3, other arithmetic: 1.76 us -> 2.38 us
where the time goes in v2:
time: 62.2 us; the launch traced here: 61.4 us
  Pallas kernels  55.1 us (89%)
  other arithmetic  3.77 us (6%)
  matrix products  2.37 us (4%)
    pallas_call x1, Pallas kernels, local(): pl.pallas_call(functools.partial(kernel, (n_chan, n_vox, per_dev, bins, o...  55.1 us
    dot_general x1, matrix products, local(): lax.dot_general(summed, kernels, (((0, 2), (0, 1)), ((), ())), preferred_...  2.37 us
    another operation x2, other arithmetic  1.76 us

profile of v2, /device:TPU:0, one launch (start us, length us, event | category | flops | bytes accessed | tf_op | source)
XLA Modules:
  0.0 61.4 jit_solution(7206315890666565260)
XLA Ops:
  0.0 0.0 copy-start
  0.0 0.7 %compare_bitcast_fusion = pred[2]{0:T(512)(128)(4,1)S(1)} fusion(s32[1,2]{1,0:T(1,128)} %param.7), kind=kLoop, calls=%fused_computation.28 | loop fusion | flops 2 | bytes 10 | tf_op jit(solution)/shard_map/gt | solution.py:271
  0.8 0.8 %fusion.7 = (bf16[32,2,32]{2,0,1:T(8,128)(2,1)S(1)}, bf16[32,2,32]{2,0,1:T(8,128)(2,1)S(1)}) fusion(s32[1,2,32,32]{3,2,1,0:T(8,128)} %param.8, pred[2]{0:T(512)(128)(4,1)S(1)} %compare_bitcast_fusion), kind=kLoop, calls=%fused_computation.21 | loop fusion | flops 45056 | bytes 16386 | tf_op jit(solution)/shard_map/convert.3
  1.6 0.1 stack.16
  1.7 0.1 stack.17
  1.8 0.9 %fusion.4 = (bf16[1,16,2048]{2,1,0:T(8,128)(2,1)S(1)}, bf16[1,16,2048]{2,1,0:T(8,128)(2,1)S(1)}) fusion(bf16[2,16,2048]{2,1,0:T(8,128)(2,1)} %param.6), kind=kLoop, calls=%fused_computation.9 | loop fusion | flops 327680 | bytes 262144 | tf_op jit(solution)/shard_map/convert.5
  2.7 0.6 %pad_maximum_fusion = (bf16[2,16,1024]{2,1,0:T(8,128)(2,1)}, bf16[2,16,1024]{2,1,0:T(8,128)(2,1)S(1)}) fusion(bf16[1,16,2048]{2,1,0:T(8,128)(2,1)S(1)} %get-tuple-element.7, bf16[1,16,2048]{2,1,0:T(8,128)(2,1)S(1)} %get-tuple-element.8), kind=kLoop, calls=%fused_computation.14 | loop fusion | flops 262144 | bytes 262144 | tf_op jit(solution)/shard_map/stack | solution.py:20
  3.4 0.6 %maximum_maximum_fusion.refs_0_ = bf16[2,16,1152]{2,1,0:T(8,128)(2,1)} fusion(bf16[1,16,128]{2,1,0:T(8,128)(2,1)S(1)} %stack.17, bf16[1,16,128]{2,1,0:T(8,128)(2,1)S(1)} %stack.16, bf16[2,16,1024]{2,1,0:T(8,128)(2,1)S(1)} %get-tuple-element.6), kind=kLoop, calls=%fused_computation.12 | loop fusion | flops 221184 | bytes 147456 | tf_op jit(solution)/shard_map/concatenate | solution.py:277
  4.0 55.1 %shard_map.64 = bf16[4,256,512]{2,1,0:T(8,128)(2,1)} custom-call(bf16[2,16,1152]{2,1,0:T(8,128)(2,1)} %maximum_maximum_fusion.refs_0_, bf16[2,16,1024]{2,1,0:T(8,128)(2,1)} %get-tuple-element.5.refs_1_, s32[4,8,256]{2,1,0:T(8,128)} %bitcast.35, bf16[4096,512]{1,0:T(8,128)(2,1)} %constant.36.clone.refs_3_), custom_call_target="tpu_custom_call" | custom-call | tf_op jit(solution)/shard_map/pallas_call | solution.py:282
  59.1 0.0 copy-done
  59.1 2.4 %convolution_bitcast_fusion = f32[256,256]{1,0:T(8,128)} fusion(bf16[4,256,512]{2,1,0:T(8,128)(2,1)} %shard_map.64, bf16[4,512,256]{2,1,0:T(8,128)(2,1)S(1)} %copy-done), kind=kOutput, calls=%fused_computation | convolution fusion | flops 268435456 | bytes 2359296 | tf_op jit(solution)/shard_map/dot_general | solution.py:306
  (2 shorter events, 0.0 us)
Async XLA Ops:
  0.0 59.1 %copy-start = (bf16[4,512,256]{2,1,0:T(8,128)(2,1)S(1)}, bf16[4,512,256]{2,1,0:T(8,128)(2,1)}, u32[]{:S(2)}) copy-start(bf16[4,512,256]{2,1,0:T(8,128)(2,1)} %param.10) | copy-start | bytes 3145732

commit v3 on v2

--- a/solution.py
+++ b/solution.py
@@ -172,7 +172,7 @@
 
     def form(stage, passing):
         per_group = width // chunk
-        steps = 4 * depth // ((n_chan // 2) * per_group)
+        steps = 2 * depth // ((n_chan // 2) * per_group)
 
         def one_group(g, carry):
             if stage == 0:
@@ -183,10 +183,10 @@
             for c in range(per_group):
                 at = c * chunk
                 re, im = channels(stage, 0, g, at), channels(stage, 1, g, at)
-                re_i = jnp.dot(pick_i, re, preferred_element_type=jnp.float32)
-                im_i = jnp.dot(pick_i, im, preferred_element_type=jnp.float32)
-                re_j = jnp.dot(pick_j, re, preferred_element_type=jnp.float32)
-                im_j = jnp.dot(pick_j, im, preferred_element_type=jnp.float32)
+                re_i = jnp.dot(pick_i, re, preferred_element_type=jnp.float32).astype(jnp.bfloat16)
+                im_i = jnp.dot(pick_i, im, preferred_element_type=jnp.float32).astype(jnp.bfloat16)
+                re_j = jnp.dot(pick_j, re, preferred_element_type=jnp.float32).astype(jnp.bfloat16)
+                im_j = jnp.dot(pick_j, im, preferred_element_type=jnp.float32).astype(jnp.bfloat16)
                 cross_re = (re_i * re_j + im_i * im_j).astype(jnp.bfloat16)
                 cross_im = (im_i * re_j - re_i * im_j).astype(jnp.bfloat16)
                 f = stage * width + at
@@ -196,19 +196,11 @@
                 )
                 if passing:
                     step = (g * per_group + c) * steps
-                    for phase in range(4):
-                        @pl.when(step // depth == phase)
+                    for phase in (2, 3):
+                        @pl.when(step // depth == phase - 2)
                         def _():
                             for i in range(steps):
-                                d = lax.rem(step, depth) + i
-                                if phase > 0:
-                                    pass_on(stage + 1, phase, d)
-                                elif i > 0:
-                                    pass_on(stage + 1, 0, d)
-                                else:
-                                    @pl.when(d > 0)
-                                    def _():
-                                        pass_on(stage + 1, 0, d)
+                                pass_on(stage + 1, phase, lax.rem(step, depth) + i)
             if stage > 0:
                 total += partial[pl.ds(base, group_rows), :]
             if stage < stages - 1:
@@ -234,6 +226,12 @@
                     pass_on(0, 0, d)
             else:
                 pass_on(0, phase, d)
+            if phase == 2:
+                @pl.when(d > 0)
+                def _():
+                    pass_on(1, 0, d)
+            if phase == 3:
+                pass_on(1, 1, d)
             count_piece(phase * depth + d)
             return carry
         lax.fori_loop(0, depth, one, 0)

time: 62.2 us -> 63.4 us (1.019)
  Pallas kernels: 55.1 us -> 56.8 us
    pallas_call x1, Pallas kernels: 55.1 us -> 56.8 us  [local(): pl.pallas_call(functools.partial(kernel, (n_chan, n_vox, per_dev, bins, o...]
where the time goes in v3:
time: 63.4 us; the launch traced here: 63.1 us
  Pallas kernels  56.8 us (90%)
  other arithmetic  3.77 us (6%)
  matrix products  2.37 us (4%)
    pallas_call x1, Pallas kernels, local(): pl.pallas_call(functools.partial(kernel, (n_chan, n_vox, per_dev, bins, o...  56.8 us
    dot_general x1, matrix products, local(): lax.dot_general(summed, kernels, (((0, 2), (0, 1)), ((), ())), preferred_...  2.37 us
    another operation x2, other arithmetic  1.76 us

profile of v3, /device:TPU:0, one launch (start us, length us, event | category | flops | bytes accessed | tf_op | source)
XLA Modules:
  0.0 63.1 jit_solution(17501082840130435663)
XLA Ops:
  0.0 0.0 copy-start
  0.0 0.7 %compare_bitcast_fusion = pred[2]{0:T(512)(128)(4,1)S(1)} fusion(s32[1,2]{1,0:T(1,128)} %param.7), kind=kLoop, calls=%fused_computation.28 | loop fusion | flops 2 | bytes 10 | tf_op jit(solution)/shard_map/gt | solution.py:269
  0.8 0.8 %fusion.7 = (bf16[32,2,32]{2,0,1:T(8,128)(2,1)S(1)}, bf16[32,2,32]{2,0,1:T(8,128)(2,1)S(1)}) fusion(s32[1,2,32,32]{3,2,1,0:T(8,128)} %param.8, pred[2]{0:T(512)(128)(4,1)S(1)} %compare_bitcast_fusion), kind=kLoop, calls=%fused_computation.21 | loop fusion | flops 45056 | bytes 16386 | tf_op jit(solution)/shard_map/convert.3
  1.6 0.1 stack.16
  1.7 0.1 stack.17
  1.8 0.9 %fusion.4 = (bf16[1,16,2048]{2,1,0:T(8,128)(2,1)S(1)}, bf16[1,16,2048]{2,1,0:T(8,128)(2,1)S(1)}) fusion(bf16[2,16,2048]{2,1,0:T(8,128)(2,1)} %param.6), kind=kLoop, calls=%fused_computation.9 | loop fusion | flops 327680 | bytes 262144 | tf_op jit(solution)/shard_map/convert.5
  2.7 0.6 pad_maximum_fusion
  3.4 0.6 %maximum_maximum_fusion.refs_0_ = bf16[2,16,1152]{2,1,0:T(8,128)(2,1)} fusion(bf16[1,16,128]{2,1,0:T(8,128)(2,1)S(1)} %stack.17, bf16[1,16,128]{2,1,0:T(8,128)(2,1)S(1)} %stack.16, bf16[2,16,1024]{2,1,0:T(8,128)(2,1)S(1)} %get-tuple-element.6), kind=kLoop, calls=%fused_computation.12 | loop fusion | flops 221184 | bytes 147456 | tf_op jit(solution)/shard_map/concatenate | solution.py:275
  4.0 56.8 %shard_map.64 = bf16[4,256,512]{2,1,0:T(8,128)(2,1)} custom-call(bf16[2,16,1152]{2,1,0:T(8,128)(2,1)} %maximum_maximum_fusion.refs_0_, bf16[2,16,1024]{2,1,0:T(8,128)(2,1)} %get-tuple-element.5.refs_1_, s32[4,8,256]{2,1,0:T(8,128)} %bitcast.35, bf16[4096,512]{1,0:T(8,128)(2,1)} %constant.36.clone.refs_3_), custom_call_target="tpu_custom_call" | custom-call | tf_op jit(solution)/shard_map/pallas_call | solution.py:280
  60.8 0.0 copy-done
  60.8 2.4 %convolution_bitcast_fusion = f32[256,256]{1,0:T(8,128)} fusion(bf16[4,256,512]{2,1,0:T(8,128)(2,1)} %shard_map.64, bf16[4,512,256]{2,1,0:T(8,128)(2,1)S(1)} %copy-done), kind=kOutput, calls=%fused_computation | convolution fusion | flops 268435456 | bytes 2359296 | tf_op jit(solution)/shard_map/dot_general | solution.py:304
  (2 shorter events, 0.0 us)
Async XLA Ops:
  0.0 60.8 %copy-start = (bf16[4,512,256]{2,1,0:T(8,128)(2,1)S(1)}, bf16[4,512,256]{2,1,0:T(8,128)(2,1)}, u32[]{:S(2)}) copy-start(bf16[4,512,256]{2,1,0:T(8,128)(2,1)} %param.10) | copy-start | bytes 3145732
